TPU v7x, 32 devices: a whole 2x2x4 slice. The times are simulated.
32 devices in a mesh: row: 4 (over y, x), col: 8 (over z, core).
Axes of the slice: x: 2, y: 2, z: 4, core: 2. Of those that a mesh axis runs over, the one named last changes fastest.
Arguments:
- chol: bfloat16 [6000, 8192], P('row', 'col'), may hold values from -1.75 to 1.75
- amplitudes: bfloat16 [8192, 4096], P('col', 'row'), may hold values from -0.0625 to 0.0625
- pair_offsets: int32 [4], replicated, may hold values from 0 to 8064
Outputs:
- residual: float32 [512, 4096], P('col', 'row')
All inputs are finite; a program needn't handle non-finite values.
Results may differ from a plain program's by a relative error of at most 0.003.
Values may be sent and summed in bfloat16 or wider, within the bound.
No kernel may reach another device: no remote copies, remote signals or barrier semaphores. Data moves between devices by JAX's collectives and lax.ppermute only.
A program may use at most 64 MiB of HBM per device.

v0:
```python
import jax
import jax.numpy as jnp
from jax import lax
from jax.sharding import PartitionSpec as P

AB_TILE = 128


def on_device(chol, amplitudes, pair_offsets):
    width = chol.shape[1]
    tile = AB_TILE
    offsets = jnp.arange(tile, dtype=jnp.int32)
    rows = (pair_offsets[:, None] + offsets[None, :]).reshape(-1)
    first = lax.axis_index("col") * width
    local_ids = first + jnp.arange(width, dtype=jnp.int32)
    selector = (local_ids[:, None] == rows[None, :]).astype(jnp.bfloat16)
    picked = jnp.dot(chol, selector, preferred_element_type=jnp.float32)
    factors = lax.psum(picked.astype(jnp.bfloat16), "col")
    partial_block = jnp.dot(factors.T, chol, preferred_element_type=jnp.float32)
    integrals = lax.psum(partial_block, "row").astype(jnp.bfloat16)
    return lax.psum_scatter(
        jnp.dot(integrals, amplitudes, preferred_element_type=jnp.float32),
        "col",
        scatter_dimension=0,
        tiled=True,
    )


def solution(mesh):
    placed = (P("row", "col"), P("col", "row"), P())
    return jax.shard_map(
        on_device, mesh=mesh, in_specs=placed, out_specs=P("col", "row"), check_vma=False
    )
```

profile of v0, /device:TPU:0, one launch (start us, length us, event | category | flops | bytes accessed | tf_op | source)
XLA Modules:
  0.0 200.8 jit_solution(691630656585019255)
XLA Ops:
  6.5 0.0 copy-start
  6.5 0.0 all-reduce.3.cloned.1.call-start
  6.5 0.9 add_bitcast_fusion
  7.4 1.0 copy-done
  8.4 3.2 %fusion = bf16[1500,512]{0,1:T(8,128)(2,1)} fusion(bf16[1500,1024]{1,0:T(8,128)(2,1)S(1)} %copy-done, s32[512]{0:T(512)S(1)} %add_bitcast_fusion, s32[1024]{0:T(1024)S(1)} %iota_add_fusion), kind=kOutput, calls=%fused_computation.1 | convolution fusion | flops 1574680576 | bytes 4614144 | tf_op jit(solution)/shard_map/dot_general | solution.py:17
  11.7 0.0 all-reduce.3.cloned.1.call-update
  11.7 0.0 reduce-scatter.2.cloned.1.call-start
  11.7 64.9 %all-reduce.3.cloned.1.call-done = bf16[1500,512]{0,1:T(8,128)(2,1)} async-done(((bf16[1500,512]{0,1:T(8,128)(2,1)}), bf16[1500,512]{0,1:T(8,128)(2,1)}) %all-reduce.3.cloned.1.call-update) | async-done | bytes 1536016 | tf_op jit(solution)/shard_map/psum | solution.py:18
  76.7 4.5 %fusion.5 = f32[512,1024]{1,0:T(8,128)} fusion(bf16[1500,512]{0,1:T(8,128)(2,1)} %all-reduce.3.cloned.1.call-done, bf16[1500,1024]{1,0:T(8,128)(2,1)S(1)} %copy-done), kind=kOutput, calls=%fused_computation.9 | convolution fusion | flops 1572864000 | bytes 6705152 | tf_op jit(solution)/shard_map/dot_general | solution.py:19
  81.2 72.7 %all-reduce.4 = bf16[512,1024]{1,0:T(8,128)(2,1)} all-reduce(f32[512,1024]{1,0:T(8,128)} %fusion.5), channel_id=1, replica_groups=mesh['row'=4,'col'=8] {'row'}, use_global_device_ids=true, to_apply=%region_1.0 | all-reduce | flops 524288 | bytes 3145728 | tf_op jit(solution)/shard_map/psum | solution.py:20
  153.9 4.5 %fusion.6 = f32[512,1024]{1,0:T(8,128)} fusion(bf16[512,1024]{1,0:T(8,128)(2,1)} %all-reduce.4, bf16[1024,1024]{1,0:T(8,128)(2,1)} %param.4), kind=kOutput, calls=%fused_computation.10 | convolution fusion | flops 1073741824 | bytes 5242880 | tf_op jit(solution)/shard_map/dot_general | solution.py:22
  158.4 0.0 reduce-scatter.2.cloned.1.call-update
  158.4 35.5 %reduce-scatter.2.cloned.1.call-done = f32[64,1024]{1,0:T(8,128)} async-done(((f32[512,1024]{1,0:T(8,128)}), f32[64,1024]{1,0:T(8,128)}) %reduce-scatter.2.cloned.1.call-update) | async-done | bytes 262160 | tf_op jit(solution)/shard_map/reduce_scatter | solution.py:21
  (1 shorter events, 0.0 us)
Async XLA Ops:
  6.5 1.9 copy-start
  6.5 70.1 %all-reduce.3.cloned.1.call-start = ((), (), s32[]{:S(2)}) async-start(), calls=%async_computation.1 | async-start | bytes 3145728 | tf_op jit(solution)/shard_map/psum | solution.py:18
  11.7 182.2 %reduce-scatter.2.cloned.1.call-start = ((), (), s32[]{:S(2)}) async-start(), calls=%async_computation.2 | async-start | bytes 2359296 | tf_op jit(solution)/shard_map/reduce_scatter | solution.py:21
Sparse Core Ops, SparseCore 0:
  11.8 64.7 all-reduce.2
  158.6 35.3 reduce-scatter.1
where the time goes:
time: 201 us
  waiting for transfers between devices  100 us (50%)
  blocking collectives  72.7 us (36%)
  between operations  13.4 us (7%)
  matrix products  12.3 us (6%)
    psum x1, blocking collectives, on_device(): integrals = lax.psum(partial_block, 'row').astype(jnp.bfloat16)  72.7 us
    psum x1, waiting for transfers between devices, on_device(): factors = lax.psum(picked.astype(jnp.bfloat16), 'col')  64.9 us
    reduce_scatter x1, waiting for transfers between devices, on_device(): lax.psum_scatter(jnp.dot(integrals, amplitudes, preferred_element_type=jn...  35.5 us
    dot_general x1, matrix products, on_device(): partial_block = jnp.dot(factors.T, chol, preferred_element_type=jnp.float32)  4.55 us
    dot_general x1, matrix products, on_device(): jnp.dot(integrals, amplitudes, preferred_element_type=jnp.float32)  4.52 us
  transfers between devices with their start and end apart: 2, of which 2 were waited for; matrix products, arithmetic and copies ran while one was open for 0% of the time, Pallas kernels for 0%

commit v1 on v0

v1 whole, which is shorter than its diff:
```python
import jax
import jax.numpy as jnp
from jax import lax
from jax.sharding import PartitionSpec as P

AB_TILE = 128
CHUNKS = 2


def pairs(rows, cols, target):
    listed = []
    for row in range(rows):
        for col in range(cols):
            to = target(row, col // 2, col % 2)
            if to is not None:
                listed.append((row * cols + col, to[0] * cols + to[1] * 2 + to[2]))
    return listed


def pick(scalars, index):
    value = scalars[0]
    for place in range(1, len(scalars)):
        value = jnp.where(index == place, scalars[place], value)
    return value


def total(terms):
    value = terms[0]
    for term in terms[1:]:
        value = value + term
    return value


def flow(owners, places):
    upto = [total([(o <= p).astype(jnp.int32) for o in owners]) for p in range(places)]
    first = [jnp.int32(0)]
    for p in range(1, places):
        first.append(jnp.maximum(0, first[-1] + 1 - (upto[p] - upto[p - 1])))
    return upto, first


def make(rows, cols):
    places = cols // 2
    bits = rows.bit_length() - 1
    swap_core = pairs(rows, cols, lambda r, z, k: (r, z, 1 - k))
    along = pairs(
        rows, cols, lambda r, z, k: (r, z + 1 - 2 * k, k) if 0 <= z + 1 - 2 * k < places else None
    )
    in_plane = [
        pairs(rows, cols, lambda r, z, k, j=j: (r ^ (1 << (j if k == 0 else bits - 1 - j)), z, k))
        for j in range(bits)
    ]
    shifts = [
        pairs(rows, cols, lambda r, z, k, s=s: (r, (z + s) % places, k)) for s in range(places)
    ]
    axes = ("row", "col")

    def on_device(chol, amplitudes, pair_offsets):
        depth, width = chol.shape
        blocks = pair_offsets.shape[0]
        share = blocks * AB_TILE // cols
        part = share // CHUNKS
        unit = AB_TILE // CHUNKS
        row, col = lax.axis_index("row"), lax.axis_index("col")
        z, core = col // 2, col % 2

        offsets = [pair_offsets[b] for b in range(blocks)]
        ahead = [
            total(
                [
                    (offsets[c] < offsets[b] if c > b else offsets[c] <= offsets[b]).astype(jnp.int32)
                    for c in range(blocks)
                    if c != b
                ]
            )
            for b in range(blocks)
        ]
        chip = 2 * width
        up = flow([o // chip for o in offsets], places)
        down = flow([places - 1 - (o + AB_TILE - 1) // chip for o in offsets], places)
        position = jnp.where(core == 0, z, places - 1 - z)
        upto = [jnp.where(core == 0, a, b) for a, b in zip(up[0], down[0])]
        first = [jnp.where(core == 0, a, b) for a, b in zip(up[1], down[1])]
        rank = [jnp.where(core == 0, blocks - 1 - a, a) for a in ahead]
        need = jnp.int32(0)
        for counts, starts in (up, down):
            for p in range(places - 1):
                need = jnp.maximum(need, counts[p] + starts[p])

        def sent(p, slot):
            q = blocks - pick(upto, p) + slot - pick(first, p)
            good = (slot >= pick(first, p)) & (q < blocks) & (p >= 0)
            b = total([jnp.where(rank[b] == q, b, 0) for b in range(blocks)])
            return jnp.where(good, b, blocks)

        local = col * width + lax.broadcasted_iota(jnp.int32, (1, width), 1)
        own = []
        for h in range(CHUNKS):
            place = jnp.arange(AB_TILE, dtype=jnp.int32).reshape(-1, CHUNKS, part)[:, h].reshape(-1)
            wanted = (pair_offsets[:, None] + place[None, :]).reshape(-1, 1)
            selector = (local == wanted).astype(jnp.bfloat16)
            own.append(
                lax.dot_general(
                    selector, chol, (((1,), (1,)), ((), ())), preferred_element_type=jnp.float32
                ).astype(jnp.bfloat16)
            )
        own = [o + lax.ppermute(o, axes, swap_core) for o in own]
        own = [o.reshape(blocks, unit, depth) for o in own]

        def rest(slots):
            came = [jnp.zeros((blocks + 1, unit, depth), jnp.bfloat16) for _ in range(CHUNKS)]
            for slot in range(slots):
                b = jnp.minimum(sent(position, slot), blocks - 1)
                r = sent(position - 1, slot)
                for h in range(CHUNKS):
                    payload = lax.dynamic_index_in_dim(own[h], b, 0, False)
                    if slot > 0:
                        payload = payload + lax.dynamic_index_in_dim(came[h], b, 0, False)
                    got = lax.ppermute(payload, axes, along)
                    came[h] = lax.dynamic_update_index_in_dim(came[h], got, r, 0)
            done = []
            for h in range(CHUNKS):
                mine = came[h][:blocks]
                factors = own[h] + mine + lax.ppermute(mine, axes, swap_core)
                factors = factors.reshape(blocks * unit, depth)
                block = jnp.dot(factors, chol, preferred_element_type=jnp.float32)
                turns = []
                for j in range(bits):
                    bit = jnp.where(core == 0, j, bits - 1 - j)
                    turn = (row >> bit) & 1
                    turns.append(turn)
                    halves = block.reshape(2, -1, width)
                    give = lax.dynamic_index_in_dim(halves, 1 - turn, 0, False)
                    keep = lax.dynamic_index_in_dim(halves, turn, 0, False)
                    block = keep + lax.ppermute(give, axes, in_plane[j])
                block = block.astype(jnp.bfloat16)
                for j in reversed(range(bits)):
                    got = lax.ppermute(block, axes, in_plane[j])
                    low = jnp.where(turns[j] == 0, block, got)
                    high = jnp.where(turns[j] == 0, got, block)
                    block = jnp.concatenate([low, high], 0)
                result = jnp.dot(block, amplitudes, preferred_element_type=jnp.float32)
                result = result.reshape(places, 2, part, -1)
                give = lax.dynamic_index_in_dim(result, 1 - core, 1, False)
                keep = lax.dynamic_index_in_dim(result, core, 1, False)
                result = keep + lax.ppermute(give, axes, swap_core)
                sums = lax.dynamic_index_in_dim(result, z, 0, False)
                for s in range(1, places):
                    to = lax.rem(z + s, places)
                    give = lax.dynamic_index_in_dim(result, to, 0, False).astype(jnp.bfloat16)
                    sums = sums + lax.ppermute(give, axes, shifts[s]).astype(jnp.float32)
                done.append(sums)
            return jnp.concatenate(done, 0)

        most = blocks + places - 2
        short = min(blocks, most)
        return lax.cond(need <= short, lambda: rest(short), lambda: rest(most))

    return on_device


def solution(mesh):
    placed = (P("row", "col"), P("col", "row"), P())
    body = make(mesh.shape["row"], mesh.shape["col"])
    return jax.shard_map(
        body, mesh=mesh, in_specs=placed, out_specs=P("col", "row"), check_vma=False
    )
```

time: 201 us -> 152 us (0.76)
  blocking collectives: 72.7 us -> 0 us
  waiting for transfers between devices: 100 us -> 32.4 us
  starting transfers between devices: 0.04 us -> 51 us
  local copies, waits for them, and re-layouts: 1.01 us -> 18.4 us
  other arithmetic: 0.88 us -> 13.9 us
  between operations: 13.4 us -> 24.3 us
  matrix products: 12.3 us -> 10.2 us
    psum x1 -> x0, blocking collectives: 72.7 us -> none  [on_device(): integrals = lax.psum(partial_block, 'row').astype(jnp.bfloat16)]
    psum x1 -> x0, waiting for transfers between devices: 64.9 us -> none  [on_device(): factors = lax.psum(picked.astype(jnp.bfloat16), 'col')]
    ppermute x0 -> x28, starting transfers between devices: none -> 51 us  [the longest x8 30.8 us: rest(): got = lax.ppermute(payload, axes, along)]
    reduce_scatter x1 -> x0, waiting for transfers between devices: 35.5 us -> none  [on_device(): lax.psum_scatter(jnp.dot(integrals, amplitudes, preferred_element_type=jn...]
    ppermute x0 -> x28, waiting for transfers between devices: none -> 32.4 us  [the longest x4 13.5 us: rest(): block = keep + lax.ppermute(give, axes, in_plane[j])]
    add x2 -> x18, other arithmetic: 0.88 us -> 11.6 us  [the longest x2 3.11 us: on_device(): own = [o + lax.ppermute(o, axes, swap_core) for o in own]]
    another operation x0 -> x6, local copies, waits for them, and re-layouts: none -> 8.23 us
    cond x0 -> x18, local copies, waits for them, and re-layouts: none -> 3.88 us
  transfers between devices with their start and end apart: 2 -> 28, of which waited for: 2 -> 11; matrix products, arithmetic and copies ran while one was open for 0% -> 18% of each run, Pallas kernels for 0% -> 0%
where the time goes in v1:
time: 152 us; the launch traced here: 151 us
  starting transfers between devices  51 us (34%)
  waiting for transfers between devices  32.4 us (21%)
  between operations  24.3 us (16%)
  local copies, waits for them, and re-layouts  18.4 us (12%)
  other arithmetic  13.9 us (9%)
  matrix products  10.2 us (7%)
    ppermute x8, starting transfers between devices, rest(): got = lax.ppermute(payload, axes, along)  30.8 us
    ppermute x4, waiting for transfers between devices, rest(): block = keep + lax.ppermute(give, axes, in_plane[j])  13.5 us
    ppermute x6, starting transfers between devices, rest(): sums = sums + lax.ppermute(give, axes, shifts[s]).astype(jnp.float32)  8.87 us
    another operation x6, local copies, waits for them, and re-layouts  8.23 us
    dot_general x2, matrix products, on_device(): lax.dot_general(selector, chol, (((1,), (1,)), ((), ())), preferred_eleme...  6.86 us
    ppermute x8, waiting for transfers between devices, rest(): got = lax.ppermute(payload, axes, along)  6.64 us
    ppermute x4, waiting for transfers between devices, rest(): got = lax.ppermute(block, axes, in_plane[j])  6.49 us
    ppermute x6, waiting for transfers between devices, rest(): sums = sums + lax.ppermute(give, axes, shifts[s]).astype(jnp.float32)  5.76 us
  transfers between devices with their start and end apart: 28, of which 11 were waited for; matrix products, arithmetic and copies ran while one was open for 18% of the time, Pallas kernels for 0%

profile of v1, /device:TPU:0, one launch (start us, length us, event | category | flops | bytes accessed | tf_op | source)
XLA Modules:
  0.0 151.4 jit_solution(10543658727306858877)
XLA Ops:
  0.2 0.7 broadcast_add_fusion
  1.0 3.0 %convolution_convert_fusion.1 = bf16[256,1500]{0,1:T(8,128)(2,1)S(1)} fusion(bf16[1500,1024]{1,0:T(8,128)(2,1)} %param.5, s32[1024]{0:T(1024)S(1)} %iota_add_fusion, s32[256]{0:T(256)S(1)} %add.933), kind=kOutput, calls=%fused_computation.159 | convolution fusion | flops 787078144 | bytes 3845120 | tf_op jit(solution)/shard_map/dot_general | solution.py:103
  4.0 0.5 collective-permute-start.56
  4.6 3.9 %convolution_convert_fusion = bf16[256,1500]{0,1:T(8,128)(2,1)} fusion(bf16[1500,1024]{1,0:T(8,128)(2,1)} %param.5, s32[1024]{0:T(1024)S(1)} %iota_add_fusion, s32[256]{0:T(256)S(1)} %add.937), kind=kOutput, calls=%fused_computation.158 | convolution fusion | flops 787078144 | bytes 3845120 | tf_op jit(solution)/shard_map/dot_general | solution.py:103
  8.6 0.6 fusion.59
  33.5 117.2 %conditional.1 = (f32[64,1024]{1,0:T(8,128)S(1)}) conditional(s32[]{:T(128)} %convert_element_type.281, (pred[]{:T(512)}, s32[]{:T(128)}, bf16[256,1500]{0,1:T(8,128)(2,1)S(1)}, bf16[256,1500]{0,1:T(8,128)(2,1)}, s32[]{:T(128)}, /*index=5*/s32[]{:T(128)}, pred[]{:T(512)}, s32[]{:T(128)}, s32[]{:T(128)}, s32[]{:T(128)}, /*index=10*/s32[]{:T(128)}, ...), branch_computations={%region_0.1_spmd, %region_1.2_spmd} | conditional | flops 2656096000 | bytes 144160256 | solution.py:157
  33.8 1.2 copy.24
  35.0 2.3 %copy.25 = bf16[256,1500]{1,0:T(8,128)(2,1)} copy(bf16[256,1500]{0,1:T(8,128)(2,1)} %get-tuple-element.568) | data formatting | bytes 1536000 | tf_op jit(solution)/shard_map
  37.3 1.6 %add.778 = bf16[256,1500]{1,0:T(8,128)(2,1)S(1)} add(bf16[256,1500]{1,0:T(8,128)(2,1)} %copy.24, bf16[256,1500]{1,0:T(8,128)(2,1)} %copy.25) | non-fusion elementwise | flops 384000 | bytes 2304000 | tf_op jit(solution)/shard_map/add | solution.py:107
  38.9 0.8 dynamic-slice_bitcast_fusion.15
  39.7 4.8 %collective-permute-start.30 = (bf16[64,1500]{1,0:T(8,128)(2,1)}, bf16[64,1500]{1,0:T(8,128)(2,1)S(1)}, u32[]{:S(2)}, u32[]{:S(2)}) collective-permute-start(bf16[64,1500]{1,0:T(8,128)(2,1)} %dynamic-slice_bitcast_fusion.15), channel_id=1, source_target_pairs={{0,2},{2,4},{3,1},{4,6},{5,3},{7,5},{8,10},{10,12},{11,9},{12,14},... | collective-permute-start | bytes 576008 | tf_op jit(solution)/shard_map/cond/branch_1_fun/ppermute | solution.py:119
  44.5 2.3 %copy.26 = bf16[256,1500]{1,0:T(8,128)(2,1)} copy(bf16[256,1500]{0,1:T(8,128)(2,1)} %get-tuple-element.601) | data formatting | bytes 1536000 | tf_op jit(solution)/shard_map
  46.8 2.3 %copy.27 = bf16[256,1500]{1,0:T(8,128)(2,1)} copy(bf16[256,1500]{0,1:T(8,128)(2,1)} %get-tuple-element.602) | data formatting | bytes 1536000 | tf_op jit(solution)/shard_map
  49.1 1.6 %add.853 = bf16[256,1500]{1,0:T(8,128)(2,1)S(1)} add(bf16[256,1500]{1,0:T(8,128)(2,1)} %copy.26, bf16[256,1500]{1,0:T(8,128)(2,1)} %copy.27) | non-fusion elementwise | flops 384000 | bytes 2304000 | tf_op jit(solution)/shard_map/add | solution.py:107
  50.6 0.9 copy-done.8
  51.6 3.5 %collective-permute-start.43 = (bf16[64,1500]{1,0:T(8,128)(2,1)S(1)}, bf16[64,1500]{1,0:T(8,128)(2,1)S(1)}, u32[]{:S(2)}, u32[]{:S(2)}) collective-permute-start(bf16[64,1500]{1,0:T(8,128)(2,1)S(1)} %dynamic-slice_bitcast_fusion.14), channel_id=1, source_target_pairs={{0,2},{2,4},{3,1},{4,6},{5,3},{7,5},{8,10},{10,12},{11,9},{12,14},... | collective-permute-start | bytes 576008 | tf_op jit(solution)/shard_map/cond/branch_1_fun/ppermute | solution.py:119
  55.4 3.6 %collective-permute-start.31 = (bf16[64,1500]{1,0:T(8,128)(2,1)S(1)}, bf16[64,1500]{1,0:T(8,128)(2,1)S(1)}, u32[]{:S(2)}, u32[]{:S(2)}) collective-permute-start(bf16[64,1500]{1,0:T(8,128)(2,1)S(1)} %add_bitcast_fusion.15), channel_id=1, source_target_pairs={{0,2},{2,4},{3,1},{4,6},{5,3},{7,5},{8,10},{10,12},{11,9},{12,14},... | collective-permute-start | bytes 576008 | tf_op jit(solution)/shard_map/cond/branch_1_fun/ppermute | solution.py:119
  59.2 3.5 %collective-permute-start.44 = (bf16[64,1500]{1,0:T(8,128)(2,1)S(1)}, bf16[64,1500]{1,0:T(8,128)(2,1)S(1)}, u32[]{:S(2)}, u32[]{:S(2)}) collective-permute-start(bf16[64,1500]{1,0:T(8,128)(2,1)S(1)} %add_bitcast_fusion.12), channel_id=1, source_target_pairs={{0,2},{2,4},{3,1},{4,6},{5,3},{7,5},{8,10},{10,12},{11,9},{12,14},... | collective-permute-start | bytes 576008 | tf_op jit(solution)/shard_map/cond/branch_1_fun/ppermute | solution.py:119
  62.8 1.0 add_bitcast_fusion.14
  63.8 3.8 %collective-permute-start.32 = (bf16[64,1500]{1,0:T(8,128)(2,1)S(1)}, bf16[64,1500]{1,0:T(8,128)(2,1)S(1)}, u32[]{:S(2)}, u32[]{:S(2)}) collective-permute-start(bf16[64,1500]{1,0:T(8,128)(2,1)S(1)} %add_bitcast_fusion.14), channel_id=1, source_target_pairs={{0,2},{2,4},{3,1},{4,6},{5,3},{7,5},{8,10},{10,12},{11,9},{12,14},... | collective-permute-start | bytes 576008 | tf_op jit(solution)/shard_map/cond/branch_1_fun/ppermute | solution.py:119
  67.7 2.7 %collective-permute-start.45 = (bf16[64,1500]{1,0:T(8,128)(2,1)S(1)}, bf16[64,1500]{1,0:T(8,128)(2,1)S(1)}, u32[]{:S(2)}, u32[]{:S(2)}) collective-permute-start(bf16[64,1500]{1,0:T(8,128)(2,1)S(1)} %add_bitcast_fusion.11), channel_id=1, source_target_pairs={{0,2},{2,4},{3,1},{4,6},{5,3},{7,5},{8,10},{10,12},{11,9},{12,14},... | collective-permute-start | bytes 576008 | tf_op jit(solution)/shard_map/cond/branch_1_fun/ppermute | solution.py:119
  70.4 0.4 collective-permute-done.32
  70.8 1.0 add_bitcast_fusion.13
  71.7 4.4 %collective-permute-start.33 = (bf16[64,1500]{1,0:T(8,128)(2,1)S(1)}, bf16[64,1500]{1,0:T(8,128)(2,1)S(1)}, u32[]{:S(2)}, u32[]{:S(2)}) collective-permute-start(bf16[64,1500]{1,0:T(8,128)(2,1)S(1)} %add_bitcast_fusion.13), channel_id=1, source_target_pairs={{0,2},{2,4},{3,1},{4,6},{5,3},{7,5},{8,10},{10,12},{11,9},{12,14},... | collective-permute-start | bytes 576008 | tf_op jit(solution)/shard_map/cond/branch_1_fun/ppermute | solution.py:119
  76.2 3.1 %collective-permute-done.33 = bf16[64,1500]{1,0:T(8,128)(2,1)S(1)} collective-permute-done((bf16[64,1500]{1,0:T(8,128)(2,1)S(1)}, bf16[64,1500]{1,0:T(8,128)(2,1)S(1)}, u32[]{:S(2)}, u32[]{:S(2)}) %collective-permute-start.33) | collective-permute-done | bytes 192032 | tf_op jit(solution)/shard_map/cond/branch_1_fun/ppermute | solution.py:119
  79.3 1.0 copy-done.2
  80.3 1.0 slice.38
  81.3 4.4 %collective-permute-start.46 = (bf16[64,1500]{1,0:T(8,128)(2,1)S(1)}, bf16[64,1500]{1,0:T(8,128)(2,1)S(1)}, u32[]{:S(2)}, u32[]{:S(2)}) collective-permute-start(bf16[64,1500]{1,0:T(8,128)(2,1)S(1)} %add_bitcast_fusion.10), channel_id=1, source_target_pairs={{0,2},{2,4},{3,1},{4,6},{5,3},{7,5},{8,10},{10,12},{11,9},{12,14},... | collective-permute-start | bytes 576008 | tf_op jit(solution)/shard_map/cond/branch_1_fun/ppermute | solution.py:119
  85.7 3.1 %collective-permute-done.46 = bf16[64,1500]{1,0:T(8,128)(2,1)S(1)} collective-permute-done((bf16[64,1500]{1,0:T(8,128)(2,1)S(1)}, bf16[64,1500]{1,0:T(8,128)(2,1)S(1)}, u32[]{:S(2)}, u32[]{:S(2)}) %collective-permute-start.46) | collective-permute-done | bytes 192032 | tf_op jit(solution)/shard_map/cond/branch_1_fun/ppermute | solution.py:119
  89.1 1.7 %add_add_fusion.3 = bf16[4,64,1500]{2,1,0:T(8,128)(2,1)S(1)} fusion(bf16[4,64,1500]{2,1,0:T(8,128)(2,1)} %collective-permute-done.34, bf16[4,64,1500]{2,1,0:T(8,128)(2,1)} %bitcast.251, bf16[5,64,1500]{2,1,0:T(8,128)(2,1)} %copy-done.2), kind=kLoop, calls=%fused_computation.88 | loop fusion | flops 768000 | bytes 3072000 | tf_op jit(solution)/shard_map/cond/branch_1_fun/add | solution.py:124
  90.9 1.0 fusion.28
  91.9 1.0 copy-done.15
  92.9 0.8 dynamic-slice_bitcast_fusion.11
  93.7 1.5 collective-permute-start.35
  95.4 1.0 fusion.26
  96.3 1.0 copy-done.17
  97.4 0.6 collective-permute-start.48
  98.0 5.2 %collective-permute-done.35 = f32[128,1024]{1,0:T(8,128)} collective-permute-done((f32[128,1024]{1,0:T(8,128)}, f32[128,1024]{1,0:T(8,128)}, u32[]{:S(2)}, u32[]{:S(2)}) %collective-permute-start.35) | collective-permute-done | bytes 524320 | tf_op jit(solution)/shard_map/cond/branch_1_fun/ppermute | solution.py:135
  103.2 1.3 bitcast_add_fusion.11
  104.5 1.6 %collective-permute-start.36 = (f32[64,1024]{1,0:T(8,128)S(1)}, f32[64,1024]{1,0:T(8,128)}, u32[]{:S(2)}, u32[]{:S(2)}) collective-permute-start(f32[64,1024]{1,0:T(8,128)S(1)} %dynamic-slice_bitcast_fusion.13), channel_id=1, source_target_pairs={{0,16},{1,9},{2,18},{3,11},{4,20},{5,13},{6,22},{7,15},{8,24},{9,1... | collective-permute-start | bytes 786440 | tf_op jit(solution)/shard_map/cond/branch_1_fun/ppermute | solution.py:135
  106.1 4.7 %collective-permute-done.48 = f32[128,1024]{1,0:T(8,128)} collective-permute-done((f32[128,1024]{1,0:T(8,128)S(1)}, f32[128,1024]{1,0:T(8,128)}, u32[]{:S(2)}, u32[]{:S(2)}) %collective-permute-start.48) | collective-permute-done | bytes 524320 | tf_op jit(solution)/shard_map/cond/branch_1_fun/ppermute | solution.py:135
  110.8 1.3 bitcast_add_fusion.9
  112.0 0.7 dynamic-slice_bitcast_fusion.12
  112.8 1.5 %collective-permute-start.49 = (f32[64,1024]{1,0:T(8,128)}, f32[64,1024]{1,0:T(8,128)}, u32[]{:S(2)}, u32[]{:S(2)}) collective-permute-start(f32[64,1024]{1,0:T(8,128)} %dynamic-slice_bitcast_fusion.12), channel_id=1, source_target_pairs={{0,16},{1,9},{2,18},{3,11},{4,20},{5,13},{6,22},{7,15},{8,24},{9,1... | collective-permute-start | bytes 786440 | tf_op jit(solution)/shard_map/cond/branch_1_fun/ppermute | solution.py:135
  114.3 1.0 fusion.39
  115.3 0.6 collective-permute-start.37
  115.9 3.6 %collective-permute-done.49 = f32[64,1024]{1,0:T(8,128)} collective-permute-done((f32[64,1024]{1,0:T(8,128)}, f32[64,1024]{1,0:T(8,128)}, u32[]{:S(2)}, u32[]{:S(2)}) %collective-permute-start.49) | collective-permute-done | bytes 262176 | tf_op jit(solution)/shard_map/cond/branch_1_fun/ppermute | solution.py:135
  119.5 1.0 fusion.38
  120.4 1.6 %collective-permute-start.50 = (bf16[64,1024]{1,0:T(8,128)(2,1)S(1)}, bf16[64,1024]{1,0:T(8,128)(2,1)S(1)}, u32[]{:S(2)}, u32[]{:S(2)}) collective-permute-start(bf16[64,1024]{1,0:T(8,128)(2,1)S(1)} %fusion.38), channel_id=1, source_target_pairs={{0,16},{1,9},{2,18},{3,11},{4,20},{5,13},{6,22},{7,15},{8,24},{9,1... | collective-permute-start | bytes 393224 | tf_op jit(solution)/shard_map/cond/branch_1_fun/ppermute | solution.py:138
  122.1 1.6 %collective-permute-start.38 = (bf16[128,1024]{1,0:T(8,128)(2,1)S(1)}, bf16[128,1024]{1,0:T(8,128)(2,1)S(1)}, u32[]{:S(2)}, u32[]{:S(2)}) collective-permute-start(bf16[128,1024]{1,0:T(8,128)(2,1)S(1)} %pad_maximum_fusion.3), channel_id=1, source_target_pairs={{0,8},{1,17},{2,10},{3,19},{4,12},{5,21},{6,14},{7,23},{8,0},{9,25... | collective-permute-start | bytes 786440 | tf_op jit(solution)/shard_map/cond/branch_1_fun/ppermute | solution.py:138
  123.7 3.3 %collective-permute-done.50 = bf16[64,1024]{1,0:T(8,128)(2,1)S(1)} collective-permute-done((bf16[64,1024]{1,0:T(8,128)(2,1)S(1)}, bf16[64,1024]{1,0:T(8,128)(2,1)S(1)}, u32[]{:S(2)}, u32[]{:S(2)}) %collective-permute-start.50) | collective-permute-done | bytes 131104 | tf_op jit(solution)/shard_map/cond/branch_1_fun/ppermute | solution.py:138
  127.0 1.5 collective-permute-start.51
  128.6 0.7 fusion.30
  129.4 0.9 dynamic-slice_bitcast_fusion.10
  130.3 3.2 %collective-permute-done.51 = bf16[128,1024]{1,0:T(8,128)(2,1)S(1)} collective-permute-done((bf16[128,1024]{1,0:T(8,128)(2,1)S(1)}, bf16[128,1024]{1,0:T(8,128)(2,1)S(1)}, u32[]{:S(2)}, u32[]{:S(2)}) %collective-permute-start.51) | collective-permute-done | bytes 262176 | tf_op jit(solution)/shard_map/cond/branch_1_fun/ppermute | solution.py:138
  133.6 0.7 fusion.34
  134.5 1.3 bitcast_add_fusion.10
  135.8 2.4 %collective-permute-start.40 = (bf16[32,1024]{1,0:T(8,128)(2,1)S(1)}, bf16[32,1024]{1,0:T(8,128)(2,1)S(1)}, u32[]{:S(2)}, u32[]{:S(2)}) collective-permute-start(bf16[32,1024]{1,0:T(8,128)(2,1)S(1)} %get-tuple-element.619), channel_id=1, source_target_pairs={{0,2},{1,3},{2,4},{3,5},{4,6},{5,7},{6,0},{7,1},{8,10},{9,11},{10,... | collective-permute-start | bytes 196616 | tf_op jit(solution)/shard_map/cond/branch_1_fun/ppermute | solution.py:151
  138.2 2.4 %collective-permute-start.42 = (bf16[32,1024]{1,0:T(8,128)(2,1)S(1)}, bf16[32,1024]{1,0:T(8,128)(2,1)S(1)}, u32[]{:S(2)}, u32[]{:S(2)}) collective-permute-start(bf16[32,1024]{1,0:T(8,128)(2,1)S(1)} %get-tuple-element.620), channel_id=1, source_target_pairs={{0,6},{1,7},{2,0},{3,1},{4,2},{5,3},{6,4},{7,5},{8,14},{9,15},{10,... | collective-permute-start | bytes 196616 | tf_op jit(solution)/shard_map/cond/branch_1_fun/ppermute | solution.py:151
  140.8 2.5 %collective-permute-start.54 = (bf16[32,1024]{1,0:T(8,128)(2,1)S(1)}, bf16[32,1024]{1,0:T(8,128)(2,1)S(1)}, u32[]{:S(2)}, u32[]{:S(2)}) collective-permute-start(bf16[32,1024]{1,0:T(8,128)(2,1)S(1)} %get-tuple-element.626), channel_id=1, source_target_pairs={{0,4},{1,5},{2,6},{3,7},{4,0},{5,1},{6,2},{7,3},{8,12},{9,13},{10,... | collective-permute-start | bytes 196616 | tf_op jit(solution)/shard_map/cond/branch_1_fun/ppermute | solution.py:151
  143.3 1.5 %collective-permute-start.55 = (bf16[32,1024]{1,0:T(8,128)(2,1)S(1)}, bf16[32,1024]{1,0:T(8,128)(2,1)S(1)}, u32[]{:S(2)}, u32[]{:S(2)}) collective-permute-start(bf16[32,1024]{1,0:T(8,128)(2,1)S(1)} %get-tuple-element.625), channel_id=1, source_target_pairs={{0,6},{1,7},{2,0},{3,1},{4,2},{5,3},{6,4},{7,5},{8,14},{9,15},{10,... | collective-permute-start | bytes 196616 | tf_op jit(solution)/shard_map/cond/branch_1_fun/ppermute | solution.py:151
  145.0 2.5 %collective-permute-done.53 = bf16[32,1024]{1,0:T(8,128)(2,1)S(1)} collective-permute-done((bf16[32,1024]{1,0:T(8,128)(2,1)S(1)}, bf16[32,1024]{1,0:T(8,128)(2,1)S(1)}, u32[]{:S(2)}, u32[]{:S(2)}) %collective-permute-start.53) | collective-permute-done | bytes 65568 | tf_op jit(solution)/shard_map/cond/branch_1_fun/ppermute | solution.py:151
  147.5 3.0 %collective-permute-done.54 = bf16[32,1024]{1,0:T(8,128)(2,1)S(1)} collective-permute-done((bf16[32,1024]{1,0:T(8,128)(2,1)S(1)}, bf16[32,1024]{1,0:T(8,128)(2,1)S(1)}, u32[]{:S(2)}, u32[]{:S(2)}) %collective-permute-start.54) | collective-permute-done | bytes 65568 | tf_op jit(solution)/shard_map/cond/branch_1_fun/ppermute | solution.py:151
  150.7 0.7 copy-done.18
  (83 shorter events, 2.3 us)
Async XLA Ops:
  4.0 4.7 %copy-start.19 = (s32[4]{0:T(128)S(1)}, s32[4]{0:T(128)}, u32[]{:S(2)}) copy-start(s32[4]{0:T(128)} %param.7) | copy-start | bytes 52
  4.0 29.5 %copy-start = (bf16[1024,1024]{1,0:T(8,128)(2,1)S(1)}, bf16[1024,1024]{1,0:T(8,128)(2,1)}, u32[]{:S(2)}) copy-start(bf16[1024,1024]{1,0:T(8,128)(2,1)} %param.6) | copy-start | bytes 6291460
  4.0 29.4 %collective-permute-start.56 = (bf16[256,1500]{0,1:T(8,128)(2,1)S(1)}, bf16[256,1500]{0,1:T(8,128)(2,1)}, u32[]{:S(2)}, u32[]{:S(2)}) collective-permute-start(bf16[256,1500]{0,1:T(8,128)(2,1)S(1)} %convolution_convert_fusion.1), channel_id=1, source_target_pairs={{0,1},{1,0},{2,3},{3,2},{4,5},{5,4},{6,7},{7,6},{8,9},{9,8},{10,11... | collective-permute-start | bytes 2304008 | tf_op jit(solution)/shard_map/ppermute | solution.py:107
  8.5 25.0 %collective-permute-start.57 = (bf16[256,1500]{0,1:T(8,128)(2,1)}, bf16[256,1500]{0,1:T(8,128)(2,1)}, u32[]{:S(2)}, u32[]{:S(2)}) collective-permute-start(bf16[256,1500]{0,1:T(8,128)(2,1)} %convolution_convert_fusion), channel_id=1, source_target_pairs={{0,1},{1,0},{2,3},{3,2},{4,5},{5,4},{6,7},{7,6},{8,9},{9,8},{10,11... | collective-permute-start | bytes 2304008 | tf_op jit(solution)/shard_map/ppermute | solution.py:107
  38.9 16.5 %copy-start.11 = (bf16[256,1500]{1,0:T(8,128)(2,1)}, bf16[256,1500]{1,0:T(8,128)(2,1)S(1)}, u32[]{:S(2)}) copy-start(bf16[256,1500]{1,0:T(8,128)(2,1)S(1)} %add.778) | copy-start | bytes 2304004 | tf_op jit(solution)/shard_map/cond
  39.7 15.6 %collective-permute-start.30 = (bf16[64,1500]{1,0:T(8,128)(2,1)}, bf16[64,1500]{1,0:T(8,128)(2,1)S(1)}, u32[]{:S(2)}, u32[]{:S(2)}) collective-permute-start(bf16[64,1500]{1,0:T(8,128)(2,1)} %dynamic-slice_bitcast_fusion.15), channel_id=1, source_target_pairs={{0,2},{2,4},{3,1},{4,6},{5,3},{7,5},{8,10},{10,12},{11,9},{12,14},... | collective-permute-start | bytes 576008 | tf_op jit(solution)/shard_map/cond/branch_1_fun/ppermute | solution.py:119
  50.6 0.9 copy-start.8
  51.6 7.5 %collective-permute-start.43 = (bf16[64,1500]{1,0:T(8,128)(2,1)S(1)}, bf16[64,1500]{1,0:T(8,128)(2,1)S(1)}, u32[]{:S(2)}, u32[]{:S(2)}) collective-permute-start(bf16[64,1500]{1,0:T(8,128)(2,1)S(1)} %dynamic-slice_bitcast_fusion.14), channel_id=1, source_target_pairs={{0,2},{2,4},{3,1},{4,6},{5,3},{7,5},{8,10},{10,12},{11,9},{12,14},... | collective-permute-start | bytes 576008 | tf_op jit(solution)/shard_map/cond/branch_1_fun/ppermute | solution.py:119
  55.2 3.9 %copy-start.9 = (bf16[256,1500]{1,0:T(8,128)(2,1)S(1)}, bf16[256,1500]{1,0:T(8,128)(2,1)}, u32[]{:S(2)}) copy-start(bf16[256,1500]{1,0:T(8,128)(2,1)} %copy-done.8) | copy-start | bytes 2304004 | tf_op jit(solution)/shard_map/cond
  55.4 7.3 %collective-permute-start.31 = (bf16[64,1500]{1,0:T(8,128)(2,1)S(1)}, bf16[64,1500]{1,0:T(8,128)(2,1)S(1)}, u32[]{:S(2)}, u32[]{:S(2)}) collective-permute-start(bf16[64,1500]{1,0:T(8,128)(2,1)S(1)} %add_bitcast_fusion.15), channel_id=1, source_target_pairs={{0,2},{2,4},{3,1},{4,6},{5,3},{7,5},{8,10},{10,12},{11,9},{12,14},... | collective-permute-start | bytes 576008 | tf_op jit(solution)/shard_map/cond/branch_1_fun/ppermute | solution.py:119
  59.2 8.4 %collective-permute-start.44 = (bf16[64,1500]{1,0:T(8,128)(2,1)S(1)}, bf16[64,1500]{1,0:T(8,128)(2,1)S(1)}, u32[]{:S(2)}, u32[]{:S(2)}) collective-permute-start(bf16[64,1500]{1,0:T(8,128)(2,1)S(1)} %add_bitcast_fusion.12), channel_id=1, source_target_pairs={{0,2},{2,4},{3,1},{4,6},{5,3},{7,5},{8,10},{10,12},{11,9},{12,14},... | collective-permute-start | bytes 576008 | tf_op jit(solution)/shard_map/cond/branch_1_fun/ppermute | solution.py:119
  63.8 7.0 %collective-permute-start.32 = (bf16[64,1500]{1,0:T(8,128)(2,1)S(1)}, bf16[64,1500]{1,0:T(8,128)(2,1)S(1)}, u32[]{:S(2)}, u32[]{:S(2)}) collective-permute-start(bf16[64,1500]{1,0:T(8,128)(2,1)S(1)} %add_bitcast_fusion.14), channel_id=1, source_target_pairs={{0,2},{2,4},{3,1},{4,6},{5,3},{7,5},{8,10},{10,12},{11,9},{12,14},... | collective-permute-start | bytes 576008 | tf_op jit(solution)/shard_map/cond/branch_1_fun/ppermute | solution.py:119
  67.7 8.5 %collective-permute-start.45 = (bf16[64,1500]{1,0:T(8,128)(2,1)S(1)}, bf16[64,1500]{1,0:T(8,128)(2,1)S(1)}, u32[]{:S(2)}, u32[]{:S(2)}) collective-permute-start(bf16[64,1500]{1,0:T(8,128)(2,1)S(1)} %add_bitcast_fusion.11), channel_id=1, source_target_pairs={{0,2},{2,4},{3,1},{4,6},{5,3},{7,5},{8,10},{10,12},{11,9},{12,14},... | collective-permute-start | bytes 576008 | tf_op jit(solution)/shard_map/cond/branch_1_fun/ppermute | solution.py:119
  71.7 7.6 %collective-permute-start.33 = (bf16[64,1500]{1,0:T(8,128)(2,1)S(1)}, bf16[64,1500]{1,0:T(8,128)(2,1)S(1)}, u32[]{:S(2)}, u32[]{:S(2)}) collective-permute-start(bf16[64,1500]{1,0:T(8,128)(2,1)S(1)} %add_bitcast_fusion.13), channel_id=1, source_target_pairs={{0,2},{2,4},{3,1},{4,6},{5,3},{7,5},{8,10},{10,12},{11,9},{12,14},... | collective-permute-start | bytes 576008 | tf_op jit(solution)/shard_map/cond/branch_1_fun/ppermute | solution.py:119
  79.3 1.0 copy-start.2
  81.3 7.8 %collective-permute-start.34 = (bf16[4,64,1500]{2,1,0:T(8,128)(2,1)}, bf16[4,64,1500]{2,1,0:T(8,128)(2,1)}, u32[]{:S(2)}, u32[]{:S(2)}) collective-permute-start(bf16[4,64,1500]{2,1,0:T(8,128)(2,1)} %slice.38), channel_id=1, source_target_pairs={{0,1},{1,0},{2,3},{3,2},{4,5},{5,4},{6,7},{7,6},{8,9},{9,8},{10,11... | collective-permute-start | bytes 2304008 | tf_op jit(solution)/shard_map/cond/branch_1_fun/ppermute | solution.py:124
  81.3 7.6 %collective-permute-start.46 = (bf16[64,1500]{1,0:T(8,128)(2,1)S(1)}, bf16[64,1500]{1,0:T(8,128)(2,1)S(1)}, u32[]{:S(2)}, u32[]{:S(2)}) collective-permute-start(bf16[64,1500]{1,0:T(8,128)(2,1)S(1)} %add_bitcast_fusion.10), channel_id=1, source_target_pairs={{0,2},{2,4},{3,1},{4,6},{5,3},{7,5},{8,10},{10,12},{11,9},{12,14},... | collective-permute-start | bytes 576008 | tf_op jit(solution)/shard_map/cond/branch_1_fun/ppermute | solution.py:119
  85.7 5.1 %copy-start.21 = (bf16[1500,1024]{1,0:T(8,128)(2,1)S(1)}, bf16[1500,1024]{1,0:T(8,128)(2,1)}, u32[]{:S(2)}) copy-start(bf16[1500,1024]{1,0:T(8,128)(2,1)} %get-tuple-element.428) | copy-start | bytes 9216004 | tf_op jit(solution)/shard_map/cond
  89.0 6.3 %collective-permute-start.47 = (bf16[4,64,1500]{2,1,0:T(8,128)(2,1)S(1)}, bf16[4,64,1500]{2,1,0:T(8,128)(2,1)S(1)}, u32[]{:S(2)}, u32[]{:S(2)}) collective-permute-start(bf16[4,64,1500]{2,1,0:T(8,128)(2,1)S(1)} %slice.39), channel_id=1, source_target_pairs={{0,1},{1,0},{2,3},{3,2},{4,5},{5,4},{6,7},{7,6},{8,9},{9,8},{10,11... | collective-permute-start | bytes 2304008 | tf_op jit(solution)/shard_map/cond/branch_1_fun/ppermute | solution.py:124
  90.9 4.4 %copy-start.10 = (bf16[256,1500]{1,0:T(8,128)(2,1)S(1)}, bf16[256,1500]{1,0:T(8,128)(2,1)}, u32[]{:S(2)}) copy-start(bf16[256,1500]{1,0:T(8,128)(2,1)} %copy-done.8) | copy-start | bytes 2304004 | tf_op jit(solution)/shard_map/cond
  91.9 1.0 copy-start.15
  93.7 9.5 %collective-permute-start.35 = (f32[128,1024]{1,0:T(8,128)}, f32[128,1024]{1,0:T(8,128)}, u32[]{:S(2)}, u32[]{:S(2)}) collective-permute-start(f32[128,1024]{1,0:T(8,128)} %dynamic-slice_bitcast_fusion.11), channel_id=1, source_target_pairs={{0,8},{1,17},{2,10},{3,19},{4,12},{5,21},{6,14},{7,23},{8,0},{9,25... | collective-permute-start | bytes 1572872 | tf_op jit(solution)/shard_map/cond/branch_1_fun/ppermute | solution.py:135
  96.3 1.0 copy-start.17
  97.4 13.4 %collective-permute-start.48 = (f32[128,1024]{1,0:T(8,128)S(1)}, f32[128,1024]{1,0:T(8,128)}, u32[]{:S(2)}, u32[]{:S(2)}) collective-permute-start(f32[128,1024]{1,0:T(8,128)S(1)} %dynamic-slice_bitcast_fusion.9), channel_id=1, source_target_pairs={{0,8},{1,17},{2,10},{3,19},{4,12},{5,21},{6,14},{7,23},{8,0},{9,25... | collective-permute-start | bytes 1572872 | tf_op jit(solution)/shard_map/cond/branch_1_fun/ppermute | solution.py:135
  104.5 9.8 %collective-permute-start.36 = (f32[64,1024]{1,0:T(8,128)S(1)}, f32[64,1024]{1,0:T(8,128)}, u32[]{:S(2)}, u32[]{:S(2)}) collective-permute-start(f32[64,1024]{1,0:T(8,128)S(1)} %dynamic-slice_bitcast_fusion.13), channel_id=1, source_target_pairs={{0,16},{1,9},{2,18},{3,11},{4,20},{5,13},{6,22},{7,15},{8,24},{9,1... | collective-permute-start | bytes 786440 | tf_op jit(solution)/shard_map/cond/branch_1_fun/ppermute | solution.py:135
  112.8 6.7 %collective-permute-start.49 = (f32[64,1024]{1,0:T(8,128)}, f32[64,1024]{1,0:T(8,128)}, u32[]{:S(2)}, u32[]{:S(2)}) collective-permute-start(f32[64,1024]{1,0:T(8,128)} %dynamic-slice_bitcast_fusion.12), channel_id=1, source_target_pairs={{0,16},{1,9},{2,18},{3,11},{4,20},{5,13},{6,22},{7,15},{8,24},{9,1... | collective-permute-start | bytes 786440 | tf_op jit(solution)/shard_map/cond/branch_1_fun/ppermute | solution.py:135
  115.3 6.8 %collective-permute-start.37 = (bf16[64,1024]{1,0:T(8,128)(2,1)S(1)}, bf16[64,1024]{1,0:T(8,128)(2,1)S(1)}, u32[]{:S(2)}, u32[]{:S(2)}) collective-permute-start(bf16[64,1024]{1,0:T(8,128)(2,1)S(1)} %fusion.39), channel_id=1, source_target_pairs={{0,16},{1,9},{2,18},{3,11},{4,20},{5,13},{6,22},{7,15},{8,24},{9,1... | collective-permute-start | bytes 393224 | tf_op jit(solution)/shard_map/cond/branch_1_fun/ppermute | solution.py:138
  120.4 6.5 %collective-permute-start.50 = (bf16[64,1024]{1,0:T(8,128)(2,1)S(1)}, bf16[64,1024]{1,0:T(8,128)(2,1)S(1)}, u32[]{:S(2)}, u32[]{:S(2)}) collective-permute-start(bf16[64,1024]{1,0:T(8,128)(2,1)S(1)} %fusion.38), channel_id=1, source_target_pairs={{0,16},{1,9},{2,18},{3,11},{4,20},{5,13},{6,22},{7,15},{8,24},{9,1... | collective-permute-start | bytes 393224 | tf_op jit(solution)/shard_map/cond/branch_1_fun/ppermute | solution.py:138
  122.1 6.4 %collective-permute-start.38 = (bf16[128,1024]{1,0:T(8,128)(2,1)S(1)}, bf16[128,1024]{1,0:T(8,128)(2,1)S(1)}, u32[]{:S(2)}, u32[]{:S(2)}) collective-permute-start(bf16[128,1024]{1,0:T(8,128)(2,1)S(1)} %pad_maximum_fusion.3), channel_id=1, source_target_pairs={{0,8},{1,17},{2,10},{3,19},{4,12},{5,21},{6,14},{7,23},{8,0},{9,25... | collective-permute-start | bytes 786440 | tf_op jit(solution)/shard_map/cond/branch_1_fun/ppermute | solution.py:138
  127.0 6.4 %collective-permute-start.51 = (bf16[128,1024]{1,0:T(8,128)(2,1)S(1)}, bf16[128,1024]{1,0:T(8,128)(2,1)S(1)}, u32[]{:S(2)}, u32[]{:S(2)}) collective-permute-start(bf16[128,1024]{1,0:T(8,128)(2,1)S(1)} %pad_maximum_fusion.4), channel_id=1, source_target_pairs={{0,8},{1,17},{2,10},{3,19},{4,12},{5,21},{6,14},{7,23},{8,0},{9,25... | collective-permute-start | bytes 786440 | tf_op jit(solution)/shard_map/cond/branch_1_fun/ppermute | solution.py:138
  129.4 5.0 %copy-start.13 = (f32[256,1024]{1,0:T(8,128)}, f32[256,1024]{1,0:T(8,128)S(1)}, u32[]{:S(2)}) copy-start(f32[256,1024]{1,0:T(8,128)S(1)} %fusion.30) | copy-start | bytes 3145732 | tf_op jit(solution)/shard_map/cond
  130.3 4.2 %collective-permute-start.39 = (f32[4,32,1024]{2,1,0:T(8,128)}, f32[4,32,1024]{2,1,0:T(8,128)}, u32[]{:S(2)}, u32[]{:S(2)}) collective-permute-start(f32[4,32,1024]{2,1,0:T(8,128)} %dynamic-slice_bitcast_fusion.10), channel_id=1, source_target_pairs={{0,1},{1,0},{2,3},{3,2},{4,5},{5,4},{6,7},{7,6},{8,9},{9,8},{10,11... | collective-permute-start | bytes 1572872 | tf_op jit(solution)/shard_map/cond/branch_1_fun/ppermute | solution.py:146
  134.3 6.3 %collective-permute-start.52 = (f32[4,32,1024]{2,1,0:T(8,128)S(1)}, f32[4,32,1024]{2,1,0:T(8,128)S(1)}, u32[]{:S(2)}, u32[]{:S(2)}) collective-permute-start(f32[4,32,1024]{2,1,0:T(8,128)S(1)} %dynamic-slice_bitcast_fusion.8), channel_id=1, source_target_pairs={{0,1},{1,0},{2,3},{3,2},{4,5},{5,4},{6,7},{7,6},{8,9},{9,8},{10,11... | collective-permute-start | bytes 1572872 | tf_op jit(solution)/shard_map/cond/branch_1_fun/ppermute | solution.py:146
  135.8 7.5 %collective-permute-start.40 = (bf16[32,1024]{1,0:T(8,128)(2,1)S(1)}, bf16[32,1024]{1,0:T(8,128)(2,1)S(1)}, u32[]{:S(2)}, u32[]{:S(2)}) collective-permute-start(bf16[32,1024]{1,0:T(8,128)(2,1)S(1)} %get-tuple-element.619), channel_id=1, source_target_pairs={{0,2},{1,3},{2,4},{3,5},{4,6},{5,7},{6,0},{7,1},{8,10},{9,11},{10,... | collective-permute-start | bytes 196616 | tf_op jit(solution)/shard_map/cond/branch_1_fun/ppermute | solution.py:151
  138.2 6.8 %collective-permute-start.41 = (bf16[32,1024]{1,0:T(8,128)(2,1)S(1)}, bf16[32,1024]{1,0:T(8,128)(2,1)S(1)}, u32[]{:S(2)}, u32[]{:S(2)}) collective-permute-start(bf16[32,1024]{1,0:T(8,128)(2,1)S(1)} %get-tuple-element.621), channel_id=1, source_target_pairs={{0,4},{1,5},{2,6},{3,7},{4,0},{5,1},{6,2},{7,3},{8,12},{9,13},{10,... | collective-permute-start | bytes 196616 | tf_op jit(solution)/shard_map/cond/branch_1_fun/ppermute | solution.py:151
  138.2 6.8 %collective-permute-start.42 = (bf16[32,1024]{1,0:T(8,128)(2,1)S(1)}, bf16[32,1024]{1,0:T(8,128)(2,1)S(1)}, u32[]{:S(2)}, u32[]{:S(2)}) collective-permute-start(bf16[32,1024]{1,0:T(8,128)(2,1)S(1)} %get-tuple-element.620), channel_id=1, source_target_pairs={{0,6},{1,7},{2,0},{3,1},{4,2},{5,3},{6,4},{7,5},{8,14},{9,15},{10,... | collective-permute-start | bytes 196616 | tf_op jit(solution)/shard_map/cond/branch_1_fun/ppermute | solution.py:151
  140.7 6.8 %collective-permute-start.53 = (bf16[32,1024]{1,0:T(8,128)(2,1)S(1)}, bf16[32,1024]{1,0:T(8,128)(2,1)S(1)}, u32[]{:S(2)}, u32[]{:S(2)}) collective-permute-start(bf16[32,1024]{1,0:T(8,128)(2,1)S(1)} %get-tuple-element.624), channel_id=1, source_target_pairs={{0,2},{1,3},{2,4},{3,5},{4,6},{5,7},{6,0},{7,1},{8,10},{9,11},{10,... | collective-permute-start | bytes 196616 | tf_op jit(solution)/shard_map/cond/branch_1_fun/ppermute | solution.py:151
  140.8 9.8 %collective-permute-start.54 = (bf16[32,1024]{1,0:T(8,128)(2,1)S(1)}, bf16[32,1024]{1,0:T(8,128)(2,1)S(1)}, u32[]{:S(2)}, u32[]{:S(2)}) collective-permute-start(bf16[32,1024]{1,0:T(8,128)(2,1)S(1)} %get-tuple-element.626), channel_id=1, source_target_pairs={{0,4},{1,5},{2,6},{3,7},{4,0},{5,1},{6,2},{7,3},{8,12},{9,13},{10,... | collective-permute-start | bytes 196616 | tf_op jit(solution)/shard_map/cond/branch_1_fun/ppermute | solution.py:151
  143.3 7.3 %collective-permute-start.55 = (bf16[32,1024]{1,0:T(8,128)(2,1)S(1)}, bf16[32,1024]{1,0:T(8,128)(2,1)S(1)}, u32[]{:S(2)}, u32[]{:S(2)}) collective-permute-start(bf16[32,1024]{1,0:T(8,128)(2,1)S(1)} %get-tuple-element.625), channel_id=1, source_target_pairs={{0,6},{1,7},{2,0},{3,1},{4,2},{5,3},{6,4},{7,5},{8,14},{9,15},{10,... | collective-permute-start | bytes 196616 | tf_op jit(solution)/shard_map/cond/branch_1_fun/ppermute | solution.py:151
  150.7 0.7 copy-start.18
